TPU v7x, 32 devices: a whole 2x2x4 slice. The times are simulated.
32 devices in a mesh: neuron: 8 (over z, y), trial: 4 (over x, core).
Axes of the slice: x: 2, y: 2, z: 4, core: 2. Of those that a mesh axis runs over, the one named last changes fastest.
Arguments:
- tensor: bfloat16 [8, 1024, 1024], P('trial', 'neuron'), may hold values from -1000 to 1000
- time_init: float32 [32, 1024], replicated, may hold values from -6 to 6
- trial_init: float32 [32, 8], P(None, 'trial'), may hold values from -6 to 6
Outputs:
- neuron_factor: float32 [32, 1024], P(None, 'neuron')
- time_factor: float32 [32, 1024], P(None, ('neuron', 'trial'))
- trial_factor: float32 [32, 8], P(None, 'trial')
All inputs are finite; a program needn't handle non-finite values.
Results may differ from a plain program's by a relative error of at most 0.011.
Values may be sent and summed in bfloat16 or wider, within the bound.
A program may use at most 64 MiB of HBM per device.

v0:
```python
import jax
import jax.numpy as jnp
from jax import lax
from jax.sharding import PartitionSpec as P

SWEEPS = 2


ridge_share = 0.1
tiny_eps = 1e-06


def gram_of(matrix):
    return lax.dot_general(
        matrix,
        matrix,
        (((1,), (1,)), ((), ())),
        precision=lax.Precision.HIGHEST,
        preferred_element_type=jnp.float32,
    )


def damped_solve(gram_mat, right_hand):
    order_size = gram_mat.shape[0]
    identity_mat = jnp.eye(order_size, dtype=jnp.float32)
    damped = gram_mat + ridge_share * (jnp.trace(gram_mat) / order_size) * identity_mat
    cholesky_low = jnp.linalg.cholesky(damped)
    return jax.scipy.linalg.cho_solve((cholesky_low, True), right_hand)


def per_device(tensor, time_init, trial_init):
    timepoints = tensor.shape[2]
    component_count = time_init.shape[0]
    neuron_count = tensor.shape[1] * lax.axis_size("neuron")
    devices = lax.axis_size("neuron") * lax.axis_size("trial")
    share_width = timepoints // devices
    position = lax.axis_index(("neuron", "trial"))

    def trial_gram_of(trial_cols):
        return gram_of(lax.all_gather(trial_cols, "trial", axis=1, tiled=True))

    trial_now = trial_init
    trial_gram = trial_gram_of(trial_now)
    time_gram = gram_of(time_init)
    time_rounded = time_init.astype(jnp.bfloat16)
    time_out = lax.dynamic_slice_in_dim(time_init, position * share_width, share_width, 1)
    neuron_now = jnp.zeros((component_count, tensor.shape[1]), jnp.float32)
    for sweep_index in range(SWEEPS):
        projected = jnp.einsum(
            "rj,kij->kri", time_rounded, tensor, preferred_element_type=jnp.float32
        )
        local_terms = jnp.sum(trial_now.T[:, :, None] * projected, axis=0)
        neuron_terms = lax.psum(local_terms, "trial")
        neuron_raw = damped_solve(trial_gram * time_gram, neuron_terms)
        raw_gram, raw_terms = lax.psum(
            (gram_of(neuron_raw), jnp.sum(neuron_raw[None] * projected, axis=2).T), "neuron"
        )
        scaling = 1.0 / jnp.sqrt(jnp.diagonal(raw_gram) / neuron_count + tiny_eps)
        neuron_now = neuron_raw * scaling[:, None]
        neuron_gram = raw_gram * scaling[:, None] * scaling[None, :]
        trial_terms = raw_terms * scaling[:, None]
        trial_now = damped_solve(neuron_gram * time_gram, trial_terms)
        trial_gram = trial_gram_of(trial_now)
        weights = (neuron_now[None] * trial_now.T[:, :, None]).astype(jnp.bfloat16)
        time_local = jnp.einsum("kri,kij->rj", weights, tensor, preferred_element_type=jnp.float32)
        time_system = neuron_gram * trial_gram
        time_terms = lax.psum(time_local, ("neuron", "trial"))
        time_raw = damped_solve(time_system, time_terms)
        time_now = time_raw / jnp.sqrt(
            jnp.mean(time_raw * time_raw, axis=1, keepdims=True) + tiny_eps
        )
        time_gram = gram_of(time_now)
        time_rounded = time_now.astype(jnp.bfloat16)
        time_out = lax.dynamic_slice_in_dim(time_now, position * share_width, share_width, 1)
    return (neuron_now, time_out, trial_now)


def solution(mesh):
    placed = (P("trial", "neuron", None), P(), P(None, "trial"))
    return jax.shard_map(
        per_device,
        mesh=mesh,
        in_specs=placed,
        out_specs=(P(None, "neuron"), P(None, ("neuron", "trial")), P(None, "trial")),
        check_vma=False,
    )
```

profile of v0, /device:TPU:0, one launch (start us, length us, event | category | flops | bytes accessed | tf_op | source)
XLA Modules:
  0.0 408.2 jit_solution(10179933881106593388)
XLA Ops:
  7.3 1.3 fusion.58
  8.5 6.1 %all-gather = f32[4,2,32]{2,1,0:T(2,128)S(1)} all-gather(f32[1,2,32]{2,1,0:T(2,128)S(1)} %bitcast.135), channel_id=1, replica_groups=mesh['neuron'=8,'trial'=4] {'trial'}, dimensions={0}, use_global_device_ids=true | all-gather | bytes 1280 | tf_op jit(solution)/shard_map/all_gather | solution.py:40
  14.7 0.8 select_reduce_fusion.8
  16.2 2.9 cholesky.104
  19.2 0.6 compare_reduce_fusion.5
  19.8 0.7 fusion.5
  20.5 2.4 custom-call.24
  23.2 11.9 %psum.56 = f32[32,128]{1,0:T(8,128)S(1)} all-reduce(f32[32,128]{1,0:T(8,128)S(1)} %get-tuple-element.13), channel_id=1, replica_groups=mesh['neuron'=8,'trial'=4] {'trial'}, use_global_device_ids=true, to_apply=%region_4.6 | all-reduce | flops 4096 | bytes 32768 | tf_op jit(solution)/shard_map/psum | solution.py:53
  35.8 37.4 %all-reduce.1 = (f32[32,32]{0,1:T(8,128)S(1)}, f32[32,2]{0,1:T(2,128)S(1)}) all-reduce(f32[32,32]{0,1:T(8,128)S(1)} %fusion.59, f32[32,2]{0,1:T(2,128)S(1)} %bitcast.137), channel_id=1, replica_groups=mesh['neuron'=8,'trial'=4] {'neuron'}, use_global_device_ids=true, to_apply=%region_5.8 | all-reduce | flops 1088 | bytes 8704 | tf_op jit(solution)/shard_map/psum | solution.py:55
  73.2 0.7 gather_fusion
  73.9 0.7 select_reduce_fusion.7
  75.4 2.9 cholesky.115
  78.4 0.6 compare_reduce_fusion.4
  79.0 0.7 fusion.6
  79.7 2.5 custom-call.25
  82.4 0.9 convolution_bitcast_fusion.1
  83.4 5.1 %all-gather.1 = f32[4,2,32]{2,1,0:T(2,128)S(1)} all-gather(f32[1,2,32]{2,1,0:T(2,128)S(1)} %bitcast.131), channel_id=1, replica_groups=mesh['neuron'=8,'trial'=4] {'trial'}, dimensions={0}, use_global_device_ids=true | all-gather | bytes 1280 | tf_op jit(solution)/shard_map/all_gather | solution.py:40
  88.5 0.8 select_reduce_fusion.6
  90.1 2.9 cholesky.126
  93.1 0.6 compare_reduce_fusion.3
  93.7 0.7 fusion.7
  94.4 2.4 custom-call.26
  96.8 105.7 %all-reduce.5.cloned.1.call-done = f32[32,1024]{1,0:T(8,128)} async-done(((f32[32,1024]{1,0:T(8,128)}), f32[32,1024]{1,0:T(8,128)}) %all-reduce.5.cloned.1.call-update) | async-done | bytes 131088 | tf_op jit(solution)/shard_map/psum | solution.py:67
  202.5 1.2 fusion.28
  203.8 0.4 multiply_reduce_fusion.1
  204.1 0.9 select_reduce_fusion.5
  206.1 2.9 cholesky.137
  209.1 0.6 compare_reduce_fusion.2
  209.7 0.7 fusion.8
  210.4 2.4 custom-call.27
  212.8 10.2 %psum.60 = f32[32,128]{1,0:T(8,128)S(1)} all-reduce(f32[32,128]{1,0:T(8,128)S(1)} %get-tuple-element.21), channel_id=1, replica_groups=mesh['neuron'=8,'trial'=4] {'trial'}, use_global_device_ids=true, to_apply=%region_14.19 | all-reduce | flops 4096 | bytes 32768 | tf_op jit(solution)/shard_map/psum | solution.py:53
  223.6 36.2 %all-reduce = (f32[32,32]{0,1:T(8,128)S(1)}, f32[32,2]{0,1:T(2,128)S(1)}) all-reduce(f32[32,32]{0,1:T(8,128)S(1)} %fusion.60, f32[32,2]{0,1:T(2,128)S(1)} %bitcast.138), channel_id=1, replica_groups=mesh['neuron'=8,'trial'=4] {'neuron'}, use_global_device_ids=true, to_apply=%region_15.20 | all-reduce | flops 1088 | bytes 8704 | tf_op jit(solution)/shard_map/psum | solution.py:55
  259.8 0.7 gather_fusion.1
  260.6 0.7 select_reduce_fusion.4
  262.1 2.9 cholesky.148
  265.0 0.6 compare_reduce_fusion.1
  265.7 0.7 fusion.9
  266.3 2.4 custom-call.28
  269.1 5.1 %all-gather.2 = f32[4,2,32]{2,1,0:T(2,128)S(1)} all-gather(f32[1,2,32]{2,1,0:T(2,128)S(1)} %bitcast.133), channel_id=1, replica_groups=mesh['neuron'=8,'trial'=4] {'trial'}, dimensions={0}, use_global_device_ids=true | all-gather | bytes 1280 | tf_op jit(solution)/shard_map/all_gather | solution.py:40
  274.2 0.8 select_reduce_fusion.3
  275.7 2.9 cholesky.159
  278.7 0.6 compare_reduce_fusion
  279.3 0.9 convolution_bitcast_fusion
  280.2 0.7 fusion.10
  280.9 2.4 custom-call.29
  283.3 115.7 %all-reduce.7.cloned.1.call-done = f32[32,1024]{1,0:T(8,128)} async-done(((f32[32,1024]{1,0:T(8,128)}), f32[32,1024]{1,0:T(8,128)}) %all-reduce.7.cloned.1.call-update) | async-done | bytes 131088 | tf_op jit(solution)/shard_map/psum | solution.py:67
  399.1 1.2 fusion.13
  400.7 0.7 dynamic-slice_divide_fusion
  (60 shorter events, 3.9 us)
Async XLA Ops:
  7.2 15.8 %copy-start = (bf16[2,128,1024]{2,1,0:T(8,128)(2,1)S(1)}, bf16[2,128,1024]{2,1,0:T(8,128)(2,1)}, u32[]{:S(2)}) copy-start(bf16[2,128,1024]{2,1,0:T(8,128)(2,1)} %param.10) | copy-start | bytes 1572868
  7.2 195.4 %all-reduce.5.cloned.1.call-start = ((), (), s32[]{:S(2)}) async-start(), calls=%async_computation | async-start | bytes 262144 | tf_op jit(solution)/shard_map/psum | solution.py:67
  7.2 1.3 copy-start.4
  8.5 14.4 %copy-start.1 = (f32[32,1024]{1,0:T(8,128)S(1)}, f32[32,1024]{1,0:T(8,128)}, u32[]{:S(2)}) copy-start(f32[32,1024]{1,0:T(8,128)} %param.11) | copy-start | bytes 393220
  83.4 315.7 %all-reduce.7.cloned.1.call-start = ((), (), s32[]{:S(2)}) async-start(), calls=%async_computation.1 | async-start | bytes 262144 | tf_op jit(solution)/shard_map/psum | solution.py:67
  260.6 18.7 %copy-start.2 = (f32[32,128]{1,0:T(8,128)}, f32[32,128]{1,0:T(8,128)S(1)}, u32[]{:S(2)}) copy-start(f32[32,128]{1,0:T(8,128)S(1)} %broadcast_multiply_fusion) | copy-start | bytes 49156
  269.1 10.2 %copy-start.3 = (f32[32,2]{0,1:T(2,128)}, f32[32,2]{0,1:T(2,128)S(1)}, u32[]{:S(2)}) copy-start(f32[32,2]{0,1:T(2,128)S(1)} %fusion.16) | copy-start | bytes 772
Sparse Core Ops, SparseCore 0:
  83.5 119.0 all-reduce.4
  280.4 118.6 all-reduce.6
where the time goes:
time: 409 us; the launch traced here: 408 us
  waiting for transfers between devices  221 us (54%)
  blocking collectives  112 us (27%)
  other arithmetic  42.8 us (10%)
  between operations  18.2 us (4%)
  matrix products  11.7 us (3%)
    psum x2, waiting for transfers between devices, per_device(): time_terms = lax.psum(time_local, ('neuron', 'trial'))  221 us
    psum x2, blocking collectives, per_device(): lax.psum((gram_of(neuron_raw), jnp.sum(neuron_raw[None] * projected, axis...  73.6 us
    psum x2, blocking collectives, per_device(): neuron_terms = lax.psum(local_terms, 'trial')  22.1 us
    another operation x18, other arithmetic, damped_solve(): cholesky_low = jnp.linalg.cholesky(damped)  21.6 us
    another operation x12, other arithmetic, damped_solve(): return jax.scipy.linalg.cho_solve((cholesky_low, True), right_hand)  18.5 us
    all_gather x3, blocking collectives, trial_gram_of(): return gram_of(lax.all_gather(trial_cols, 'trial', axis=1, tiled=True))  16.3 us
  transfers between devices with their start and end apart: 2, of which 2 were waited for; matrix products, arithmetic and copies ran while one was open for 3% of the time, Pallas kernels for 0%

commit v1 on v0

v1 whole, which is shorter than its diff:
```python
import functools

import jax
import jax.numpy as jnp
from jax import lax
from jax.experimental import pallas as pl
from jax.experimental.pallas import tpu as pltpu
from jax.sharding import PartitionSpec as P

SWEEPS = 2

ridge_share = 0.1
tiny_eps = 1e-06
LANES = 128
ROWS = 8
MESH = pl.DeviceIdType.MESH
EXACT = lax.Precision.HIGHEST
NT = (((1,), (1,)), ((), ()))


def each(low, high, step):
    if high - low <= 40:
        for index in range(low, high):
            step(index)
    else:

        def body(index, carry):
            step(index)
            return carry

        lax.fori_loop(low, high, body, 0)


def wait_bytes(ref, sem):
    pltpu.make_async_copy(ref, ref, sem).wait()


def kernel(
    neuron_devices,
    trial_devices,
    tensor_hbm,
    time_ref,
    trial_ref,
    neuron_out,
    time_out,
    trial_out,
    tensor_v,
    trial_all,
    proj_all,
    gram_all,
    time_local,
    time_parts,
    time_sums,
    time_keep,
    load_sem,
    trial_sem,
    send_sem,
    recv_sem,
):
    trials_here, neurons_here, timepoints = tensor_hbm.shape
    comps = time_ref.shape[0]
    devices = neuron_devices * trial_devices
    trials = trials_here * trial_devices
    neurons = neurons_here * neuron_devices
    chunks = timepoints // LANES
    groups = comps // ROWS
    tiles = chunks * groups
    units = min(devices, tiles)
    per = tiles // units
    stride = devices // units
    my_neuron = lax.axis_index("neuron")
    my_trial = lax.axis_index("trial")
    me = my_neuron * trial_devices + my_trial

    def device_of(linear):
        return (linear // trial_devices, lax.rem(linear, trial_devices))

    loads = []
    for k in range(trials_here):
        load = pltpu.make_async_copy(
            tensor_hbm.at[k],
            tensor_v.at[pl.ds(k * neurons_here, neurons_here)],
            load_sem.at[k],
        )
        load.start()
        loads.append(load)

    barrier = pltpu.get_barrier_semaphore()

    def greet(step):
        pl.semaphore_signal(
            barrier,
            inc=1,
            device_id=device_of(lax.rem(me + step, devices)),
            device_id_type=MESH,
        )

    each(1, devices, greet)

    lane = lax.broadcasted_iota(jnp.int32, (comps, LANES), 1)
    row = lax.broadcasted_iota(jnp.int32, (comps, LANES), 0)
    eye = (lane == row).astype(jnp.float32)
    right_eye = (lane == row + comps).astype(jnp.float32)
    in_gram = lane < comps
    in_right = (lane >= comps) & (lane < 2 * comps)
    in_terms = (lane >= comps) & (lane < comps + trials)

    def wide_gram(matrix):
        padded = jnp.concatenate(
            [matrix, jnp.zeros((LANES - comps, matrix.shape[1]), matrix.dtype)], axis=0
        )
        return lax.dot_general(
            matrix, padded, NT, precision=EXACT, preferred_element_type=jnp.float32
        )

    def eliminate(system):
        for k in range(0, comps, 2):
            col0 = jnp.broadcast_to(system[:, k : k + 1], (comps, LANES))
            col1 = jnp.broadcast_to(system[:, k + 1 : k + 2], (comps, LANES))
            row0 = system[k : k + 1, :]
            row1 = system[k + 1 : k + 2, :]
            a, c = col0[k : k + 1, :], col0[k + 1 : k + 2, :]
            b, d = col1[k : k + 1, :], col1[k + 1 : k + 2, :]
            inverse = 1.0 / (a * d - b * c)
            new0 = (d * row0 - b * row1) * inverse
            new1 = (a * row1 - c * row0) * inverse
            system = system - col0 * new0 - col1 * new1
            system = jnp.where(row == k, new0, jnp.where(row == k + 1, new1, system))
        return system

    def mean_trace(gram):
        return jnp.sum(
            jnp.sum(gram * eye, axis=0, keepdims=True), axis=1, keepdims=True
        ) * (1.0 / comps)

    def inverse_of(gram):
        scale = 1.0 / mean_trace(gram)
        system = eliminate((gram * scale + ridge_share * eye) + right_eye * scale)
        return jnp.where(in_right, system, 0.0)

    def apply_inverse(inverse, right_hand):
        width = right_hand.shape[1]
        padded = jnp.concatenate(
            [
                jnp.zeros((comps, width), jnp.float32),
                right_hand,
                jnp.zeros((LANES - 2 * comps, width), jnp.float32),
            ],
            axis=0,
        )
        return lax.dot_general(
            inverse,
            padded,
            (((1,), (0,)), ((), ())),
            precision=EXACT,
            preferred_element_type=jnp.float32,
        )

    def send_all(source, target, count, target_of, sends, receives):
        def start(step):
            pltpu.make_async_remote_copy(
                src_ref=source,
                dst_ref=target,
                send_sem=sends,
                recv_sem=receives,
                device_id=target_of(step),
                device_id_type=MESH,
            ).start()

        each(1, count, start)

    def trial_peer(step):
        return (my_neuron, lax.rem(my_trial + step, trial_devices))

    def neuron_peer(step):
        return (lax.rem(my_neuron + step, neuron_devices), my_trial)

    time_now = time_ref[...]
    time_rounded = time_now.astype(jnp.bfloat16)
    time_gram = wide_gram(time_now)
    placed = jnp.zeros((comps, LANES), jnp.float32)
    for k in range(trials_here):
        placed = jnp.where(
            lane == comps + my_trial * trials_here + k, trial_ref[:, k : k + 1], placed
        )
    trial_all[0] = placed

    pl.semaphore_wait(barrier, devices - 1)

    def start_trial(step):
        pltpu.make_async_remote_copy(
            src_ref=trial_all.at[0],
            dst_ref=trial_all.at[step],
            send_sem=trial_sem.at[0],
            recv_sem=trial_sem.at[1],
            device_id=trial_peer(step),
            device_id_type=MESH,
        ).start()

    each(1, trial_devices, start_trial)
    for load in loads:
        load.wait()

    trial_wide = None
    trial_gram = None
    for sweep in range(SWEEPS):
        sends = [send_sem.at[sweep, phase] for phase in range(4)]
        receives = [recv_sem.at[sweep, phase] for phase in range(4)]

        projected = lax.dot_general(
            time_rounded, tensor_v[...], NT, preferred_element_type=jnp.float32
        )
        for k in range(trials_here):
            proj_all[sweep, my_trial, k] = projected[
                :, k * neurons_here : (k + 1) * neurons_here
            ]
        mine = proj_all.at[sweep, my_trial]
        send_all(mine, mine, trial_devices, trial_peer, sends[0], receives[0])
        if sweep == 0:
            others = trial_all.at[pl.ds(1, trial_devices - 1)]
            wait_bytes(others, trial_sem.at[1])
            wait_bytes(others, trial_sem.at[0])
            trial_wide = jnp.sum(trial_all[...], axis=0)
            trial_gram = wide_gram(trial_wide)
        inverse = inverse_of(trial_gram * time_gram)
        others = proj_all.at[sweep, pl.ds(0, trial_devices - 1)]
        wait_bytes(others, receives[0])

        blocks = [
            proj_all[sweep, k // trials_here, k % trials_here] for k in range(trials)
        ]
        terms = jnp.zeros((comps, neurons_here), jnp.float32)
        for k in range(trials):
            terms = terms + trial_wide[:, comps + k : comps + k + 1] * blocks[k]
        neuron_raw = apply_inverse(inverse, terms)
        payload = wide_gram(neuron_raw)
        for k in range(trials):
            total = jnp.sum(neuron_raw * blocks[k], axis=1, keepdims=True)
            payload = jnp.where(lane == comps + k, total, payload)
        half = comps // 2
        folded = payload[:half] + pltpu.roll(payload[half:], LANES // 2, 1)
        gram_all[sweep, 0] = folded

        def start_gram(step):
            pltpu.make_async_remote_copy(
                src_ref=gram_all.at[sweep, 0],
                dst_ref=gram_all.at[sweep, step],
                send_sem=sends[1],
                recv_sem=receives[1],
                device_id=neuron_peer(step),
                device_id_type=MESH,
            ).start()

        each(1, neuron_devices, start_gram)
        wait_bytes(others, sends[0])
        others = gram_all.at[sweep, pl.ds(1, neuron_devices - 1)]
        wait_bytes(others, receives[1])
        folded = jnp.sum(gram_all[sweep], axis=0)
        payload = jnp.concatenate([folded, pltpu.roll(folded, LANES // 2, 1)], axis=0)
        raw_gram = jnp.where(in_gram, payload, 0.0)

        squares = raw_gram * eye
        down = lax.rsqrt(
            jnp.sum(squares, axis=1, keepdims=True) * (1.0 / neurons) + tiny_eps
        )
        across = lax.rsqrt(
            jnp.sum(squares, axis=0, keepdims=True) * (1.0 / neurons) + tiny_eps
        )
        neuron_now = neuron_raw * down
        neuron_gram = raw_gram * down * across
        gram = neuron_gram * time_gram
        scale = 1.0 / mean_trace(gram)
        system = jnp.where(
            in_gram,
            gram * scale + ridge_share * eye,
            jnp.where(in_terms, payload * down * scale, 0.0),
        )
        system = eliminate(system)
        trial_wide = jnp.where(in_terms, system, 0.0)
        own = [
            jnp.sum(
                jnp.where(
                    lane == comps + my_trial * trials_here + k, trial_wide, 0.0
                ),
                axis=1,
                keepdims=True,
            )
            for k in range(trials_here)
        ]

        weights = jnp.concatenate(
            [(neuron_now * own[k]).astype(jnp.bfloat16) for k in range(trials_here)],
            axis=1,
        )
        local = jnp.dot(weights, tensor_v[...], preferred_element_type=jnp.float32)
        for c in range(chunks):
            for g in range(groups):
                time_local[sweep, c * groups + g] = local[
                    g * ROWS : (g + 1) * ROWS, c * LANES : (c + 1) * LANES
                ]
        my_unit = me // stride

        def start_part(step):
            unit = lax.rem(my_unit + step, units)
            owner = unit * stride
            slot = lax.rem(owner - me + devices, devices)
            pltpu.make_async_remote_copy(
                src_ref=time_local.at[sweep, pl.ds(unit * per, per)],
                dst_ref=time_parts.at[sweep, slot],
                send_sem=sends[2],
                recv_sem=receives[2],
                device_id=device_of(owner),
                device_id_type=MESH,
            ).start()

        each(1, units, start_part)
        if stride > 1:
            pl.when(lax.rem(me, stride) != 0)(lambda: start_part(0))
        trial_gram = wide_gram(trial_wide)
        inverse = inverse_of(neuron_gram * trial_gram)
        wait_bytes(others, sends[1])

        def reduce_and_send():
            wait_bytes(time_parts.at[sweep, pl.ds(1, devices - 1)], receives[2])
            slice_here = pl.ds(my_unit * per, per)
            total = time_local[sweep, slice_here]
            total = total + jnp.sum(time_parts[sweep, pl.ds(1, devices - 1)], axis=0)
            time_sums[sweep, slice_here] = total
            mine = time_sums.at[sweep, slice_here]

            def start_sum(step):
                pltpu.make_async_remote_copy(
                    src_ref=mine,
                    dst_ref=mine,
                    send_sem=sends[3],
                    recv_sem=receives[3],
                    device_id=device_of(lax.rem(me + step, devices)),
                    device_id_type=MESH,
                ).start()

            each(1, devices, start_sum)
            some = time_sums.at[sweep, pl.ds(0, (units - 1) * per)]
            wait_bytes(some, receives[3])
            wait_bytes(some, sends[2])
            wait_bytes(time_parts.at[sweep, pl.ds(1, devices - 1)], sends[3])

        def send_only():
            wait_bytes(time_sums.at[sweep], receives[3])
            wait_bytes(time_sums.at[sweep], sends[2])

        if stride == 1:
            reduce_and_send()
        else:
            pl.when(lax.rem(me, stride) == 0)(reduce_and_send)
            pl.when(lax.rem(me, stride) != 0)(send_only)
        time_terms = jnp.concatenate(
            [
                time_sums[sweep, pl.ds(c * groups, groups)].reshape(comps, LANES)
                for c in range(chunks)
            ],
            axis=1,
        )
        time_raw = apply_inverse(inverse, time_terms)
        if sweep < SWEEPS - 1:
            raw_gram = wide_gram(time_raw)
            squares = raw_gram * eye
            down = lax.rsqrt(
                jnp.sum(squares, axis=1, keepdims=True) * (1.0 / timepoints) + tiny_eps
            )
            across = lax.rsqrt(
                jnp.sum(squares, axis=0, keepdims=True) * (1.0 / timepoints) + tiny_eps
            )
            time_gram = raw_gram * down * across
            time_rounded = (time_raw * down).astype(jnp.bfloat16)
        else:
            down = lax.rsqrt(
                jnp.sum(time_raw * time_raw, axis=1, keepdims=True)
                * (1.0 / timepoints)
                + tiny_eps
            )
            for c in range(chunks):
                time_keep[c] = time_raw[:, c * LANES : (c + 1) * LANES] * down
            share = timepoints // devices
            shares = LANES // share
            chunk = time_keep[me // shares]
            shift = lax.rem(LANES - lax.rem(me, shares) * share, LANES)
            time_out[...] = pltpu.roll(chunk, shift, 1)[:, :share]
            neuron_out[...] = neuron_now
            for k in range(trials_here):
                trial_out[:, k : k + 1] = own[k]


def per_device(neuron_devices, trial_devices, tensor, time_init, trial_init):
    trials_here, neurons_here, timepoints = tensor.shape
    comps = time_init.shape[0]
    devices = neuron_devices * trial_devices
    tiles = (timepoints // LANES) * (comps // ROWS)
    per = tiles // min(devices, tiles)
    f32 = jnp.float32
    vmem = pl.BlockSpec(memory_space=pltpu.VMEM)
    return pl.pallas_call(
        functools.partial(kernel, neuron_devices, trial_devices),
        out_shape=(
            jax.ShapeDtypeStruct((comps, neurons_here), f32),
            jax.ShapeDtypeStruct((comps, timepoints // devices), f32),
            jax.ShapeDtypeStruct((comps, trials_here), f32),
        ),
        in_specs=[pl.BlockSpec(memory_space=pl.ANY), vmem, vmem],
        out_specs=(vmem, vmem, vmem),
        scratch_shapes=[
            pltpu.VMEM((trials_here * neurons_here, timepoints), jnp.bfloat16),
            pltpu.VMEM((trial_devices, comps, LANES), f32),
            pltpu.VMEM((SWEEPS, trial_devices, trials_here, comps, neurons_here), f32),
            pltpu.VMEM((SWEEPS, neuron_devices, comps // 2, LANES), f32),
            pltpu.VMEM((SWEEPS, tiles, ROWS, LANES), f32),
            pltpu.VMEM((SWEEPS, devices, per, ROWS, LANES), f32),
            pltpu.VMEM((SWEEPS, tiles, ROWS, LANES), f32),
            pltpu.VMEM((timepoints // LANES, comps, LANES), f32),
            pltpu.SemaphoreType.DMA((trials_here,)),
            pltpu.SemaphoreType.DMA((2,)),
            pltpu.SemaphoreType.DMA((SWEEPS, 4)),
            pltpu.SemaphoreType.DMA((SWEEPS, 4)),
        ],
        compiler_params=pltpu.CompilerParams(
            collective_id=0,
            has_side_effects=True,
            vmem_limit_bytes=32 * 1024 * 1024,
        ),
    )(tensor, time_init, trial_init)


def solution(mesh):
    placed = (P("trial", "neuron", None), P(), P(None, "trial"))
    return jax.shard_map(
        functools.partial(per_device, mesh.shape["neuron"], mesh.shape["trial"]),
        mesh=mesh,
        in_specs=placed,
        out_specs=(P(None, "neuron"), P(None, ("neuron", "trial")), P(None, "trial")),
        check_vma=False,
    )
```

time: 409 us -> 59.4 us (0.15)
  waiting for transfers between devices: 221 us -> 0 us
  blocking collectives: 112 us -> 0 us
  Pallas kernels: 0 us -> 54 us
  other arithmetic: 42.8 us -> 0 us
  between operations: 18.2 us -> 0.64 us
  matrix products: 11.7 us -> 0 us
    psum x2 -> x0, waiting for transfers between devices: 221 us -> none  [per_device(): time_terms = lax.psum(time_local, ('neuron', 'trial'))]
    psum x4 -> x0, blocking collectives: 95.7 us -> none  [the longest x2 73.6 us: per_device(): lax.psum((gram_of(neuron_raw), jnp.sum(neuron_raw[None] * projected, axis...]
    pallas_call x0 -> x1, Pallas kernels: none -> 54 us  [per_device(): pl.pallas_call(functools.partial(kernel, neuron_devices, trial_devices),...]
    another operation x30 -> x0, other arithmetic: 40.1 us -> none  [the longest x18 21.6 us: damped_solve(): cholesky_low = jnp.linalg.cholesky(damped)]
    all_gather x3 -> x0, blocking collectives: 16.3 us -> none  [trial_gram_of(): return gram_of(lax.all_gather(trial_cols, 'trial', axis=1, tiled=True))]
    dot_general x11 -> x0, matrix products: 7.3 us -> none  [the longest x7 4.99 us: gram_of(): lax.dot_general(matrix, matrix, (((1,), (1,)), ((), ())), precision=lax.P...]
    another operation x12 -> x0, matrix products: 4.41 us -> none  [damped_solve(): return jax.scipy.linalg.cho_solve((cholesky_low, True), right_hand)]
  transfers between devices with their start and end apart: 2 -> 0, of which waited for: 2 -> 0; matrix products, arithmetic and copies ran while one was open for 3% -> 0% of each run, Pallas kernels for 0% -> 0%
where the time goes in v1:
time: 59.4 us; the launch traced here: 59.2 us
  Pallas kernels  54 us (91%)
  local copies, waits for them, and re-layouts  4.55 us (8%)
  between operations  0.64 us (1%)
    pallas_call x1, Pallas kernels, per_device(): pl.pallas_call(functools.partial(kernel, neuron_devices, trial_devices),...  54 us
    unnamed x7, local copies, waits for them, and re-layouts  3.91 us

profile of v1, /device:TPU:0, one launch (start us, length us, event | category | flops | bytes accessed | tf_op | source)
XLA Modules:
  0.0 59.2 jit_solution(12007564725196943936)
XLA Ops:
  0.6 0.8 %copy.6.trial_ref = f32[32,2]{1,0:T(8,128)S(1)} copy(f32[32,2]{0,1:T(2,128)} %param.5) | data formatting | bytes 512 | tf_op args[2]
  1.4 0.0 copy-start
  1.4 1.0 %copy-done = bf16[2,128,1024]{2,1,0:T(8,128)(2,1)S(1)} copy-done((bf16[2,128,1024]{2,1,0:T(8,128)(2,1)S(1)}, bf16[2,128,1024]{2,1,0:T(8,128)(2,1)}, u32[]{:S(2)}) %copy-start) | copy-done | bytes 524312
  2.4 0.0 copy-start.1
  2.4 0.9 %copy-done.1 = f32[32,1024]{1,0:T(8,128)S(1)} copy-done((f32[32,1024]{1,0:T(8,128)S(1)}, f32[32,1024]{1,0:T(8,128)}, u32[]{:S(2)}) %copy-start.1) | copy-done | bytes 131096
  3.3 54.0 %shard_map.58 = (f32[32,128]{1,0:T(8,128)S(1)}, f32[32,32]{1,0:T(8,128)S(1)}, f32[32,2]{1,0:T(8,128)S(1)}) custom-call(bf16[2,128,1024]{2,1,0:T(8,128)(2,1)S(1)} %copy-done, f32[32,1024]{1,0:T(8,128)S(1)} %copy-done.1, f32[32,2]{1,0:T(8,128)S(1)} %copy.6.trial_ref), custom_call_target="tpu_custom_call" | custom-call | tf_op jit(solution)/shard_map/pallas_call | solution.py:401
  57.4 0.6 %copy.7 = f32[32,2]{0,1:T(2,128)} copy(f32[32,2]{1,0:T(8,128)S(1)} %get-tuple-element.5) | data formatting | bytes 512 | tf_op jit(solution)/shard_map/pallas_call | solution.py:401
  58.0 0.6 %copy.10 = f32[32,128]{1,0:T(8,128)} copy(f32[32,128]{1,0:T(8,128)S(1)} %get-tuple-element.9) | data formatting | bytes 32768
  58.6 0.6 %copy.11 = f32[32,32]{1,0:T(8,128)} copy(f32[32,32]{1,0:T(8,128)S(1)} %get-tuple-element.10) | data formatting | bytes 8192
Async XLA Ops:
  1.4 1.0 %copy-start = (bf16[2,128,1024]{2,1,0:T(8,128)(2,1)S(1)}, bf16[2,128,1024]{2,1,0:T(8,128)(2,1)}, u32[]{:S(2)}) copy-start(bf16[2,128,1024]{2,1,0:T(8,128)(2,1)} %tensor_hbm.1) | copy-start | bytes 1572868
  2.4 0.9 %copy-start.1 = (f32[32,1024]{1,0:T(8,128)S(1)}, f32[32,1024]{1,0:T(8,128)}, u32[]{:S(2)}) copy-start(f32[32,1024]{1,0:T(8,128)} %time_ref.1) | copy-start | bytes 393220

commit v2 on v1

--- a/solution.py
+++ b/solution.py
@@ -39,12 +39,14 @@
     neuron_devices,
     trial_devices,
     tensor_hbm,
-    time_ref,
-    trial_ref,
+    time_hbm,
+    trial_hbm,
     neuron_out,
     time_out,
     trial_out,
     tensor_v,
+    time_ref,
+    trial_ref,
     trial_all,
     proj_all,
     gram_all,
@@ -52,13 +54,15 @@
     time_parts,
     time_sums,
     time_keep,
+    norm_all,
     load_sem,
+    norm_sem,
     trial_sem,
     send_sem,
     recv_sem,
 ):
     trials_here, neurons_here, timepoints = tensor_hbm.shape
-    comps = time_ref.shape[0]
+    comps = time_hbm.shape[0]
     devices = neuron_devices * trial_devices
     trials = trials_here * trial_devices
     neurons = neurons_here * neuron_devices
@@ -72,37 +76,63 @@
     my_trial = lax.axis_index("trial")
     me = my_neuron * trial_devices + my_trial
 
+    direct = stride == 1 and devices <= 64
+    share = timepoints // devices
+    by_columns = direct and share * groups == LANES
+    neuron_ids = [
+        lax.rem(my_neuron + step, neuron_devices)
+        for step in range(neuron_devices if direct else 0)
+    ]
+    trial_ids = [lax.rem(my_trial + step, trial_devices) for step in range(trial_devices)]
+
     def device_of(linear):
         return (linear // trial_devices, lax.rem(linear, trial_devices))
 
+    def each_other(visit):
+        if direct:
+            for slot in range(1, devices):
+                visit(
+                    slot,
+                    (
+                        neuron_ids[slot // trial_devices],
+                        trial_ids[slot % trial_devices],
+                    ),
+                )
+        else:
+            each(
+                1,
+                devices,
+                lambda step: visit(step, device_of(lax.rem(me + step, devices))),
+            )
+
+    time_load = pltpu.make_async_copy(time_hbm, time_ref, load_sem.at[0])
+    time_load.start()
+    trial_load = pltpu.make_async_copy(trial_hbm, trial_ref, load_sem.at[1])
+    trial_load.start()
     loads = []
     for k in range(trials_here):
         load = pltpu.make_async_copy(
             tensor_hbm.at[k],
             tensor_v.at[pl.ds(k * neurons_here, neurons_here)],
-            load_sem.at[k],
+            load_sem.at[2 + k],
         )
         load.start()
         loads.append(load)
 
     barrier = pltpu.get_barrier_semaphore()
 
-    def greet(step):
-        pl.semaphore_signal(
-            barrier,
-            inc=1,
-            device_id=device_of(lax.rem(me + step, devices)),
-            device_id_type=MESH,
-        )
-
-    each(1, devices, greet)
+    def greet(slot, device):
+        pl.semaphore_signal(barrier, inc=1, device_id=device, device_id_type=MESH)
+
+    each_other(greet)
 
     lane = lax.broadcasted_iota(jnp.int32, (comps, LANES), 1)
     row = lax.broadcasted_iota(jnp.int32, (comps, LANES), 0)
     eye = (lane == row).astype(jnp.float32)
-    right_eye = (lane == row + comps).astype(jnp.float32)
+    right_eye = ((lane >= comps) & (lax.rem(lane, comps) == row)).astype(jnp.float32)
     in_gram = lane < comps
-    in_right = (lane >= comps) & (lane < 2 * comps)
+    lane8 = lax.broadcasted_iota(jnp.int32, (ROWS, LANES), 1)
+    in_low = (lane >= 2 * comps) & (lane < 3 * comps)
     in_terms = (lane >= comps) & (lane < comps + trials)
 
     def wide_gram(matrix):
@@ -113,19 +143,48 @@
             matrix, padded, NT, precision=EXACT, preferred_element_type=jnp.float32
         )
 
+    def split(matrix):
+        high = matrix.astype(jnp.bfloat16)
+        return high, (matrix - high.astype(jnp.float32)).astype(jnp.bfloat16)
+
+    def split_gram(matrix):
+        high, low = split(matrix)
+        left = jnp.concatenate([high, low, high], axis=1)
+        right = jnp.concatenate([high, high, low], axis=1)
+        blank = jnp.zeros((LANES - comps, right.shape[1]), jnp.bfloat16)
+        return lax.dot_general(
+            left,
+            jnp.concatenate([right, blank], axis=0),
+            NT,
+            preferred_element_type=jnp.float32,
+        )
+
     def eliminate(system):
-        for k in range(0, comps, 2):
-            col0 = jnp.broadcast_to(system[:, k : k + 1], (comps, LANES))
-            col1 = jnp.broadcast_to(system[:, k + 1 : k + 2], (comps, LANES))
-            row0 = system[k : k + 1, :]
-            row1 = system[k + 1 : k + 2, :]
-            a, c = col0[k : k + 1, :], col0[k + 1 : k + 2, :]
-            b, d = col1[k : k + 1, :], col1[k + 1 : k + 2, :]
-            inverse = 1.0 / (a * d - b * c)
-            new0 = (d * row0 - b * row1) * inverse
-            new1 = (a * row1 - c * row0) * inverse
-            system = system - col0 * new0 - col1 * new1
-            system = jnp.where(row == k, new0, jnp.where(row == k + 1, new1, system))
+        for k in range(0, comps, 4):
+            cols = [
+                jnp.broadcast_to(system[:, k + j : k + j + 1], (comps, LANES))
+                for j in range(4)
+            ]
+            for pair in (0, 2):
+                top, low = k + pair, k + pair + 1
+                col0, col1 = cols[pair], cols[pair + 1]
+                a, c = col0[top : top + 1, :], col0[low : low + 1, :]
+                b, d = col1[top : top + 1, :], col1[low : low + 1, :]
+                inverse = 1.0 / (a * d - b * c)
+                a, b, c, d = a * inverse, b * inverse, c * inverse, d * inverse
+
+                def step(matrix):
+                    row0, row1 = matrix[top : top + 1, :], matrix[low : low + 1, :]
+                    new0 = d * row0 - b * row1
+                    new1 = a * row1 - c * row0
+                    matrix = matrix - col0 * new0 - col1 * new1
+                    return jnp.where(
+                        row == top, new0, jnp.where(row == low, new1, matrix)
+                    )
+
+                if pair == 0:
+                    cols[2], cols[3] = step(cols[2]), step(cols[3])
+                system = step(system)
         return system
 
     def mean_trace(gram):
@@ -136,23 +195,21 @@
     def inverse_of(gram):
         scale = 1.0 / mean_trace(gram)
         system = eliminate((gram * scale + ridge_share * eye) + right_eye * scale)
-        return jnp.where(in_right, system, 0.0)
+        low = system - system.astype(jnp.bfloat16).astype(jnp.float32)
+        return jnp.where(in_gram, 0.0, jnp.where(in_low, low, system)).astype(
+            jnp.bfloat16
+        )
 
     def apply_inverse(inverse, right_hand):
         width = right_hand.shape[1]
+        high, low = split(right_hand)
         padded = jnp.concatenate(
-            [
-                jnp.zeros((comps, width), jnp.float32),
-                right_hand,
-                jnp.zeros((LANES - 2 * comps, width), jnp.float32),
-            ],
-            axis=0,
+            [jnp.zeros((comps, width), jnp.bfloat16), high, high, low], axis=0
         )
         return lax.dot_general(
             inverse,
             padded,
             (((1,), (0,)), ((), ())),
-            precision=EXACT,
             preferred_element_type=jnp.float32,
         )
 
@@ -170,20 +227,26 @@
         each(1, count, start)
 
     def trial_peer(step):
-        return (my_neuron, lax.rem(my_trial + step, trial_devices))
+        return (my_neuron, trial_ids[step])
 
     def neuron_peer(step):
+        if direct:
+            return (neuron_ids[step], my_trial)
         return (lax.rem(my_neuron + step, neuron_devices), my_trial)
 
+    trial_load.wait()
+    placed = jnp.zeros((comps, LANES), jnp.float32)
+    for k in range(trials_here):
+        column = jnp.sum(
+            trial_ref[k : k + 1, :] * eye[:, :comps], axis=1, keepdims=True
+        )
+        placed = jnp.where(
+            lane == comps + my_trial * trials_here + k, column, placed
+        )
+    trial_all[0] = placed
+    time_load.wait()
     time_now = time_ref[...]
     time_rounded = time_now.astype(jnp.bfloat16)
-    time_gram = wide_gram(time_now)
-    placed = jnp.zeros((comps, LANES), jnp.float32)
-    for k in range(trials_here):
-        placed = jnp.where(
-            lane == comps + my_trial * trials_here + k, trial_ref[:, k : k + 1], placed
-        )
-    trial_all[0] = placed
 
     pl.semaphore_wait(barrier, devices - 1)
 
@@ -216,6 +279,7 @@
             ]
         mine = proj_all.at[sweep, my_trial]
         send_all(mine, mine, trial_devices, trial_peer, sends[0], receives[0])
+        time_gram = split_gram(time_now)
         if sweep == 0:
             others = trial_all.at[pl.ds(1, trial_devices - 1)]
             wait_bytes(others, trial_sem.at[1])
@@ -233,7 +297,7 @@
         for k in range(trials):
             terms = terms + trial_wide[:, comps + k : comps + k + 1] * blocks[k]
         neuron_raw = apply_inverse(inverse, terms)
-        payload = wide_gram(neuron_raw)
+        payload = split_gram(neuron_raw)
         for k in range(trials):
             total = jnp.sum(neuron_raw * blocks[k], axis=1, keepdims=True)
             payload = jnp.where(lane == comps + k, total, payload)
@@ -292,12 +356,24 @@
             [(neuron_now * own[k]).astype(jnp.bfloat16) for k in range(trials_here)],
             axis=1,
         )
+        columns = by_columns and sweep == SWEEPS - 1
         local = jnp.dot(weights, tensor_v[...], preferred_element_type=jnp.float32)
         for c in range(chunks):
             for g in range(groups):
-                time_local[sweep, c * groups + g] = local[
-                    g * ROWS : (g + 1) * ROWS, c * LANES : (c + 1) * LANES
-                ]
+                if columns:
+                    tile = None
+                    for h in range(groups):
+                        part = local[
+                            h * ROWS : (h + 1) * ROWS, c * LANES : (c + 1) * LANES
+                        ]
+                        if h != g:
+                            part = pltpu.roll(part, ((h - g) * share) % LANES, 1)
+                        tile = part if h == 0 else jnp.where(lane8 < h * share, tile, part)
+                else:
+                    tile = local[
+                        g * ROWS : (g + 1) * ROWS, c * LANES : (c + 1) * LANES
+                    ]
+                time_local[sweep, c * groups + g] = tile
         my_unit = me // stride
 
         def start_part(step):
@@ -313,7 +389,21 @@
                 device_id_type=MESH,
             ).start()
 
-        each(1, units, start_part)
+        def start_direct(slot, device):
+            unit = device[0] * trial_devices + device[1]
+            pltpu.make_async_remote_copy(
+                src_ref=time_local.at[sweep, pl.ds(unit * per, per)],
+                dst_ref=time_parts.at[sweep, slot],
+                send_sem=sends[2],
+                recv_sem=receives[2],
+                device_id=device,
+                device_id_type=MESH,
+            ).start()
+
+        if direct:
+            each_other(start_direct)
+        else:
+            each(1, units, start_part)
         if stride > 1:
             pl.when(lax.rem(me, stride) != 0)(lambda: start_part(0))
         trial_gram = wide_gram(trial_wide)
@@ -325,21 +415,24 @@
             slice_here = pl.ds(my_unit * per, per)
             total = time_local[sweep, slice_here]
             total = total + jnp.sum(time_parts[sweep, pl.ds(1, devices - 1)], axis=0)
+            some = time_sums.at[sweep, pl.ds(0, (units - 1) * per)]
+            if columns:
+                wait_bytes(some, sends[2])
+                return total.reshape(ROWS, LANES)
             time_sums[sweep, slice_here] = total
             mine = time_sums.at[sweep, slice_here]
 
-            def start_sum(step):
+            def start_sum(slot, device):
                 pltpu.make_async_remote_copy(
                     src_ref=mine,
                     dst_ref=mine,
                     send_sem=sends[3],
                     recv_sem=receives[3],
-                    device_id=device_of(lax.rem(me + step, devices)),
+                    device_id=device,
                     device_id_type=MESH,
                 ).start()
 
-            each(1, devices, start_sum)
-            some = time_sums.at[sweep, pl.ds(0, (units - 1) * per)]
+            each_other(start_sum)
             wait_bytes(some, receives[3])
             wait_bytes(some, sends[2])
             wait_bytes(time_parts.at[sweep, pl.ds(1, devices - 1)], sends[3])
@@ -348,6 +441,42 @@
             wait_bytes(time_sums.at[sweep], receives[3])
             wait_bytes(time_sums.at[sweep], sends[2])
 
+        if columns:
+            tile = reduce_and_send()
+            mine = jnp.concatenate(
+                [tile]
+                + [pltpu.roll(tile, LANES - g * share, 1) for g in range(1, groups)],
+                axis=0,
+            )
+            time_raw = apply_inverse(inverse, jnp.where(lane < share, mine, 0.0))
+            sums = jnp.sum(time_raw * time_raw, axis=1, keepdims=True)
+            norm_all[0] = jnp.sum(sums * eye, axis=0, keepdims=True)
+
+            def start_norm(slot, device):
+                pltpu.make_async_remote_copy(
+                    src_ref=norm_all.at[0],
+                    dst_ref=norm_all.at[slot],
+                    send_sem=norm_sem.at[0],
+                    recv_sem=norm_sem.at[1],
+                    device_id=device,
+                    device_id_type=MESH,
+                ).start()
+
+            each_other(start_norm)
+            neuron_out[...] = neuron_now
+            for k in range(trials_here):
+                trial_out[k : k + 1, :] = jnp.sum(
+                    own[k] * eye[:, :comps], axis=0, keepdims=True
+                )
+            others = norm_all.at[pl.ds(1, devices - 1)]
+            wait_bytes(others, norm_sem.at[1])
+            sums = jnp.sum(
+                jnp.sum(norm_all[...], axis=0) * eye, axis=1, keepdims=True
+            )
+            down = lax.rsqrt(sums * (1.0 / timepoints) + tiny_eps)
+            time_out[...] = (time_raw * down)[:, :share]
+            wait_bytes(others, norm_sem.at[0])
+            break
         if stride == 1:
             reduce_and_send()
         else:
@@ -361,33 +490,36 @@
             axis=1,
         )
         time_raw = apply_inverse(inverse, time_terms)
-        if sweep < SWEEPS - 1:
-            raw_gram = wide_gram(time_raw)
-            squares = raw_gram * eye
-            down = lax.rsqrt(
-                jnp.sum(squares, axis=1, keepdims=True) * (1.0 / timepoints) + tiny_eps
-            )
-            across = lax.rsqrt(
-                jnp.sum(squares, axis=0, keepdims=True) * (1.0 / timepoints) + tiny_eps
-            )
-            time_gram = raw_gram * down * across
-            time_rounded = (time_raw * down).astype(jnp.bfloat16)
-        else:
-            down = lax.rsqrt(
-                jnp.sum(time_raw * time_raw, axis=1, keepdims=True)
-                * (1.0 / timepoints)
-                + tiny_eps
-            )
+        down = lax.rsqrt(
+            jnp.sum(time_raw * time_raw, axis=1, keepdims=True) * (1.0 / timepoints)
+            + tiny_eps
+        )
+        time_now = time_raw * down
+        time_rounded = time_now.astype(jnp.bfloat16)
+        if sweep == SWEEPS - 1:
             for c in range(chunks):
-                time_keep[c] = time_raw[:, c * LANES : (c + 1) * LANES] * down
-            share = timepoints // devices
+                time_keep[c] = time_now[:, c * LANES : (c + 1) * LANES]
             shares = LANES // share
             chunk = time_keep[me // shares]
             shift = lax.rem(LANES - lax.rem(me, shares) * share, LANES)
             time_out[...] = pltpu.roll(chunk, shift, 1)[:, :share]
             neuron_out[...] = neuron_now
             for k in range(trials_here):
-                trial_out[:, k : k + 1] = own[k]
+                trial_out[k : k + 1, :] = jnp.sum(
+                    own[k] * eye[:, :comps], axis=0, keepdims=True
+                )
+
+
+def keep(neuron_in, time_in, trial_in, neuron_out, time_out, trial_out, sem):
+    copies = [
+        pltpu.make_async_copy(neuron_in, neuron_out, sem.at[0]),
+        pltpu.make_async_copy(time_in, time_out, sem.at[1]),
+        pltpu.make_async_copy(trial_in, trial_out, sem.at[2]),
+    ]
+    for copy in copies:
+        copy.start()
+    for copy in copies:
+        copy.wait()
 
 
 def per_device(neuron_devices, trial_devices, tensor, time_init, trial_init):
@@ -398,17 +530,19 @@
     per = tiles // min(devices, tiles)
     f32 = jnp.float32
     vmem = pl.BlockSpec(memory_space=pltpu.VMEM)
-    return pl.pallas_call(
+    results = pl.pallas_call(
         functools.partial(kernel, neuron_devices, trial_devices),
         out_shape=(
             jax.ShapeDtypeStruct((comps, neurons_here), f32),
             jax.ShapeDtypeStruct((comps, timepoints // devices), f32),
-            jax.ShapeDtypeStruct((comps, trials_here), f32),
+            jax.ShapeDtypeStruct((trials_here, comps), f32),
         ),
-        in_specs=[pl.BlockSpec(memory_space=pl.ANY), vmem, vmem],
+        in_specs=[pl.BlockSpec(memory_space=pl.ANY)] * 3,
         out_specs=(vmem, vmem, vmem),
         scratch_shapes=[
             pltpu.VMEM((trials_here * neurons_here, timepoints), jnp.bfloat16),
+            pltpu.VMEM((comps, timepoints), f32),
+            pltpu.VMEM((trials_here, comps), f32),
             pltpu.VMEM((trial_devices, comps, LANES), f32),
             pltpu.VMEM((SWEEPS, trial_devices, trials_here, comps, neurons_here), f32),
             pltpu.VMEM((SWEEPS, neuron_devices, comps // 2, LANES), f32),
@@ -416,7 +550,9 @@
             pltpu.VMEM((SWEEPS, devices, per, ROWS, LANES), f32),
             pltpu.VMEM((SWEEPS, tiles, ROWS, LANES), f32),
             pltpu.VMEM((timepoints // LANES, comps, LANES), f32),
-            pltpu.SemaphoreType.DMA((trials_here,)),
+            pltpu.VMEM((devices, 1, LANES), f32),
+            pltpu.SemaphoreType.DMA((2 + trials_here,)),
+            pltpu.SemaphoreType.DMA((2,)),
             pltpu.SemaphoreType.DMA((2,)),
             pltpu.SemaphoreType.DMA((SWEEPS, 4)),
             pltpu.SemaphoreType.DMA((SWEEPS, 4)),
@@ -424,9 +560,17 @@
         compiler_params=pltpu.CompilerParams(
             collective_id=0,
             has_side_effects=True,
-            vmem_limit_bytes=32 * 1024 * 1024,
+            vmem_limit_bytes=56 * 1024 * 1024,
         ),
-    )(tensor, time_init, trial_init)
+    )(tensor, time_init, trial_init.T)
+    neuron_now, time_now, trial_now = pl.pallas_call(
+        keep,
+        out_shape=tuple(jax.ShapeDtypeStruct(r.shape, f32) for r in results),
+        in_specs=[pl.BlockSpec(memory_space=pl.ANY)] * 3,
+        out_specs=(pl.BlockSpec(memory_space=pl.ANY),) * 3,
+        scratch_shapes=[pltpu.SemaphoreType.DMA((3,))],
+    )(*results)
+    return neuron_now, time_now, trial_now.T
 
 
 def solution(mesh):

time: 59.4 us -> 54.4 us (0.916)
  local copies, waits for them, and re-layouts: 4.55 us -> 0 us
    unnamed x7 -> x0, local copies, waits for them, and re-layouts: 3.91 us -> none
    pallas_call x1, Pallas kernels: 54 us -> 51.4 us  [per_device(): pl.pallas_call(functools.partial(kernel, neuron_devices, trial_devices),...]
    pallas_call x0 -> x1, Pallas kernels: none -> 2.15 us  [per_device(): pl.pallas_call(keep, out_shape=tuple((jax.ShapeDtypeStruct(r.shape, f32)...]
    pallas_call x1 -> x0, local copies, waits for them, and re-layouts: 0.64 us -> none  [per_device(): pl.pallas_call(functools.partial(kernel, neuron_devices, trial_devices),...]
where the time goes in v2:
time: 54.4 us; the launch traced here: 54.2 us
  Pallas kernels  53.6 us (99%)
  between operations  0.64 us (1%)
    pallas_call x1, Pallas kernels, per_device(): pl.pallas_call(functools.partial(kernel, neuron_devices, trial_devices),...  51.4 us
    pallas_call x1, Pallas kernels, per_device(): pl.pallas_call(keep, out_shape=tuple((jax.ShapeDtypeStruct(r.shape, f32)...  2.15 us

profile of v2, /device:TPU:0, one launch (start us, length us, event | category | flops | bytes accessed | tf_op | source)
XLA Modules:
  0.0 54.2 jit_solution(8663062107242767055)
XLA Ops:
  0.6 51.4 %shard_map.58 = (f32[32,128]{1,0:T(8,128)}, f32[32,32]{1,0:T(8,128)}, f32[2,32]{1,0:T(2,128)}) custom-call(bf16[2,128,1024]{2,1,0:T(8,128)(2,1)} %tensor_hbm.1, f32[32,1024]{1,0:T(8,128)} %time_hbm.1, f32[2,32]{1,0:T(2,128)} %bitcast.2), custom_call_target="tpu_custom_call" | custom-call | tf_op jit(solution)/shard_map/pallas_call | solution.py:533
  52.1 2.2 %shard_map.59 = (f32[32,128]{1,0:T(8,128)}, f32[32,32]{1,0:T(8,128)}, f32[2,32]{1,0:T(2,128)}) custom-call(f32[32,128]{1,0:T(8,128)} %get-tuple-element.9.neuron_in, f32[32,32]{1,0:T(8,128)} %get-tuple-element.10.time_in, f32[2,32]{1,0:T(2,128)} %get-tuple-element.11.trial_in), custom_call_target="tpu_custom_call" | custom-call | tf_op jit(solution)/shard_map/pallas_call | solution.py:566

commit v3 on v2

--- a/solution.py
+++ b/solution.py
@@ -52,7 +52,10 @@
     gram_all,
     time_local,
     time_parts,
-    time_sums,
+    share_local,
+    share_parts,
+    middle,
+    share_sums,
     time_keep,
     norm_all,
     load_sem,
@@ -68,15 +71,12 @@
     neurons = neurons_here * neuron_devices
     chunks = timepoints // LANES
     groups = comps // ROWS
-    tiles = chunks * groups
-    units = min(devices, tiles)
-    per = tiles // units
-    stride = devices // units
+    width = timepoints // trial_devices
     my_neuron = lax.axis_index("neuron")
     my_trial = lax.axis_index("trial")
     me = my_neuron * trial_devices + my_trial
 
-    direct = stride == 1 and devices <= 64
+    direct = devices <= 64
     share = timepoints // devices
     by_columns = direct and share * groups == LANES
     neuron_ids = [
@@ -267,8 +267,8 @@
     trial_wide = None
     trial_gram = None
     for sweep in range(SWEEPS):
-        sends = [send_sem.at[sweep, phase] for phase in range(4)]
-        receives = [recv_sem.at[sweep, phase] for phase in range(4)]
+        sends = [send_sem.at[sweep, phase] for phase in range(5)]
+        receives = [recv_sem.at[sweep, phase] for phase in range(5)]
 
         projected = lax.dot_general(
             time_rounded, tensor_v[...], NT, preferred_element_type=jnp.float32
@@ -358,9 +358,9 @@
         )
         columns = by_columns and sweep == SWEEPS - 1
         local = jnp.dot(weights, tensor_v[...], preferred_element_type=jnp.float32)
-        for c in range(chunks):
-            for g in range(groups):
-                if columns:
+        if columns:
+            for c in range(chunks):
+                for g in range(groups):
                     tile = None
                     for h in range(groups):
                         part = local[
@@ -369,80 +369,42 @@
                         if h != g:
                             part = pltpu.roll(part, ((h - g) * share) % LANES, 1)
                         tile = part if h == 0 else jnp.where(lane8 < h * share, tile, part)
-                else:
-                    tile = local[
-                        g * ROWS : (g + 1) * ROWS, c * LANES : (c + 1) * LANES
-                    ]
-                time_local[sweep, c * groups + g] = tile
-        my_unit = me // stride
-
-        def start_part(step):
-            unit = lax.rem(my_unit + step, units)
-            owner = unit * stride
-            slot = lax.rem(owner - me + devices, devices)
-            pltpu.make_async_remote_copy(
-                src_ref=time_local.at[sweep, pl.ds(unit * per, per)],
-                dst_ref=time_parts.at[sweep, slot],
-                send_sem=sends[2],
-                recv_sem=receives[2],
-                device_id=device_of(owner),
-                device_id_type=MESH,
-            ).start()
-
-        def start_direct(slot, device):
-            unit = device[0] * trial_devices + device[1]
-            pltpu.make_async_remote_copy(
-                src_ref=time_local.at[sweep, pl.ds(unit * per, per)],
-                dst_ref=time_parts.at[sweep, slot],
-                send_sem=sends[2],
-                recv_sem=receives[2],
-                device_id=device,
-                device_id_type=MESH,
-            ).start()
-
-        if direct:
-            each_other(start_direct)
+                    time_local[c * groups + g] = tile
+
+            def start_tile(slot, device):
+                pltpu.make_async_remote_copy(
+                    src_ref=time_local.at[device[0] * trial_devices + device[1]],
+                    dst_ref=time_parts.at[slot],
+                    send_sem=sends[2],
+                    recv_sem=receives[2],
+                    device_id=device,
+                    device_id_type=MESH,
+                ).start()
+
+            each_other(start_tile)
         else:
-            each(1, units, start_part)
-        if stride > 1:
-            pl.when(lax.rem(me, stride) != 0)(lambda: start_part(0))
+            for t in range(trial_devices):
+                share_local[sweep, t] = local[:, t * width : (t + 1) * width]
+
+            def start_share(step):
+                pltpu.make_async_remote_copy(
+                    src_ref=share_local.at[sweep, trial_ids[step]],
+                    dst_ref=share_parts.at[sweep, step],
+                    send_sem=sends[2],
+                    recv_sem=receives[2],
+                    device_id=trial_peer(step),
+                    device_id_type=MESH,
+                ).start()
+
+            each(1, trial_devices, start_share)
         trial_gram = wide_gram(trial_wide)
         inverse = inverse_of(neuron_gram * trial_gram)
         wait_bytes(others, sends[1])
 
-        def reduce_and_send():
-            wait_bytes(time_parts.at[sweep, pl.ds(1, devices - 1)], receives[2])
-            slice_here = pl.ds(my_unit * per, per)
-            total = time_local[sweep, slice_here]
-            total = total + jnp.sum(time_parts[sweep, pl.ds(1, devices - 1)], axis=0)
-            some = time_sums.at[sweep, pl.ds(0, (units - 1) * per)]
-            if columns:
-                wait_bytes(some, sends[2])
-                return total.reshape(ROWS, LANES)
-            time_sums[sweep, slice_here] = total
-            mine = time_sums.at[sweep, slice_here]
-
-            def start_sum(slot, device):
-                pltpu.make_async_remote_copy(
-                    src_ref=mine,
-                    dst_ref=mine,
-                    send_sem=sends[3],
-                    recv_sem=receives[3],
-                    device_id=device,
-                    device_id_type=MESH,
-                ).start()
-
-            each_other(start_sum)
-            wait_bytes(some, receives[3])
-            wait_bytes(some, sends[2])
-            wait_bytes(time_parts.at[sweep, pl.ds(1, devices - 1)], sends[3])
-
-        def send_only():
-            wait_bytes(time_sums.at[sweep], receives[3])
-            wait_bytes(time_sums.at[sweep], sends[2])
-
         if columns:
-            tile = reduce_and_send()
+            others = time_parts.at[pl.ds(1, devices - 1)]
+            wait_bytes(others, receives[2])
+            tile = time_local[me] + jnp.sum(time_parts[1:devices], axis=0)
             mine = jnp.concatenate(
                 [tile]
                 + [pltpu.roll(tile, LANES - g * share, 1) for g in range(1, groups)],
@@ -468,6 +430,7 @@
                 trial_out[k : k + 1, :] = jnp.sum(
                     own[k] * eye[:, :comps], axis=0, keepdims=True
                 )
+            wait_bytes(others, sends[2])
             others = norm_all.at[pl.ds(1, devices - 1)]
             wait_bytes(others, norm_sem.at[1])
             sums = jnp.sum(
@@ -477,19 +440,41 @@
             time_out[...] = (time_raw * down)[:, :share]
             wait_bytes(others, norm_sem.at[0])
             break
-        if stride == 1:
-            reduce_and_send()
-        else:
-            pl.when(lax.rem(me, stride) == 0)(reduce_and_send)
-            pl.when(lax.rem(me, stride) != 0)(send_only)
+
+        others = share_parts.at[sweep, pl.ds(1, trial_devices - 1)]
+        wait_bytes(others, receives[2])
+        total = share_local[sweep, my_trial]
+        for t in range(1, trial_devices):
+            total = total + share_parts[sweep, t]
+        middle[sweep, 0] = total.astype(jnp.bfloat16)
+
+        def start_middle(step):
+            pltpu.make_async_remote_copy(
+                src_ref=middle.at[sweep, 0],
+                dst_ref=middle.at[sweep, step],
+                send_sem=sends[3],
+                recv_sem=receives[3],
+                device_id=neuron_peer(step),
+                device_id_type=MESH,
+            ).start()
+
+        each(1, neuron_devices, start_middle)
+        wait_bytes(others, sends[2])
+        others = middle.at[sweep, pl.ds(1, neuron_devices - 1)]
+        wait_bytes(others, receives[3])
+        share_sums[sweep, my_trial] = jnp.sum(
+            middle[sweep].astype(jnp.float32), axis=0
+        )
+        mine = share_sums.at[sweep, my_trial]
+        send_all(mine, mine, trial_devices, trial_peer, sends[4], receives[4])
+        wait_bytes(others, sends[3])
+        others = share_sums.at[sweep, pl.ds(0, trial_devices - 1)]
+        wait_bytes(others, receives[4])
         time_terms = jnp.concatenate(
-            [
-                time_sums[sweep, pl.ds(c * groups, groups)].reshape(comps, LANES)
-                for c in range(chunks)
-            ],
-            axis=1,
+            [share_sums[sweep, t] for t in range(trial_devices)], axis=1
         )
         time_raw = apply_inverse(inverse, time_terms)
+        wait_bytes(others, sends[4])
         down = lax.rsqrt(
             jnp.sum(time_raw * time_raw, axis=1, keepdims=True) * (1.0 / timepoints)
             + tiny_eps
@@ -527,7 +512,7 @@
     comps = time_init.shape[0]
     devices = neuron_devices * trial_devices
     tiles = (timepoints // LANES) * (comps // ROWS)
-    per = tiles // min(devices, tiles)
+    shares = (SWEEPS, trial_devices, comps, timepoints // trial_devices)
     f32 = jnp.float32
     vmem = pl.BlockSpec(memory_space=pltpu.VMEM)
     results = pl.pallas_call(
@@ -546,16 +531,19 @@
             pltpu.VMEM((trial_devices, comps, LANES), f32),
             pltpu.VMEM((SWEEPS, trial_devices, trials_here, comps, neurons_here), f32),
             pltpu.VMEM((SWEEPS, neuron_devices, comps // 2, LANES), f32),
-            pltpu.VMEM((SWEEPS, tiles, ROWS, LANES), f32),
-            pltpu.VMEM((SWEEPS, devices, per, ROWS, LANES), f32),
-            pltpu.VMEM((SWEEPS, tiles, ROWS, LANES), f32),
+            pltpu.VMEM((tiles, ROWS, LANES), f32),
+            pltpu.VMEM((devices, ROWS, LANES), f32),
+            pltpu.VMEM(shares, f32),
+            pltpu.VMEM(shares, f32),
+            pltpu.VMEM((SWEEPS, neuron_devices) + shares[2:], jnp.bfloat16),
+            pltpu.VMEM(shares, f32),
             pltpu.VMEM((timepoints // LANES, comps, LANES), f32),
             pltpu.VMEM((devices, 1, LANES), f32),
             pltpu.SemaphoreType.DMA((2 + trials_here,)),
             pltpu.SemaphoreType.DMA((2,)),
             pltpu.SemaphoreType.DMA((2,)),
-            pltpu.SemaphoreType.DMA((SWEEPS, 4)),
-            pltpu.SemaphoreType.DMA((SWEEPS, 4)),
+            pltpu.SemaphoreType.DMA((SWEEPS, 5)),
+            pltpu.SemaphoreType.DMA((SWEEPS, 5)),
         ],
         compiler_params=pltpu.CompilerParams(
             collective_id=0,

time: 54.4 us -> 54 us (level)
  no operation moved by 1% of the time
where the time goes in v3:
time: 54 us; the launch traced here: 53.9 us
  Pallas kernels  53.3 us (99%)
  between operations  0.64 us (1%)
    pallas_call x1, Pallas kernels, per_device(): pl.pallas_call(functools.partial(kernel, neuron_devices, trial_devices),...  51.1 us
    pallas_call x1, Pallas kernels, per_device(): pl.pallas_call(keep, out_shape=tuple((jax.ShapeDtypeStruct(r.shape, f32)...  2.15 us

profile of v3, /device:TPU:0, one launch (start us, length us, event | category | flops | bytes accessed | tf_op | source)
XLA Modules:
  0.0 53.9 jit_solution(13415091383466940939)
XLA Ops:
  0.6 51.1 %shard_map.58 = (f32[32,128]{1,0:T(8,128)}, f32[32,32]{1,0:T(8,128)}, f32[2,32]{1,0:T(2,128)}) custom-call(bf16[2,128,1024]{2,1,0:T(8,128)(2,1)} %tensor_hbm.1, f32[32,1024]{1,0:T(8,128)} %time_hbm.1, f32[2,32]{1,0:T(2,128)} %bitcast.2), custom_call_target="tpu_custom_call" | custom-call | tf_op jit(solution)/shard_map/pallas_call | solution.py:518
  51.7 2.2 %shard_map.59 = (f32[32,128]{1,0:T(8,128)}, f32[32,32]{1,0:T(8,128)}, f32[2,32]{1,0:T(2,128)}) custom-call(f32[32,128]{1,0:T(8,128)} %get-tuple-element.9.neuron_in, f32[32,32]{1,0:T(8,128)} %get-tuple-element.10.time_in, f32[2,32]{1,0:T(2,128)} %get-tuple-element.11.trial_in), custom_call_target="tpu_custom_call" | custom-call | tf_op jit(solution)/shard_map/pallas_call | solution.py:554

commit v4 on v3

--- a/solution.py
+++ b/solution.py
@@ -160,32 +160,51 @@
         )
 
     def eliminate(system):
+        spread = (ROWS, LANES)
+        parts = [system[v * ROWS : (v + 1) * ROWS] for v in range(groups)]
+        row8 = lax.broadcasted_iota(jnp.int32, spread, 0)
         for k in range(0, comps, 4):
+            home, at = k // ROWS, k % ROWS
             cols = [
-                jnp.broadcast_to(system[:, k + j : k + j + 1], (comps, LANES))
+                [jnp.broadcast_to(part[:, k + j : k + j + 1], spread) for part in parts]
                 for j in range(4)
             ]
-            for pair in (0, 2):
-                top, low = k + pair, k + pair + 1
-                col0, col1 = cols[pair], cols[pair + 1]
-                a, c = col0[top : top + 1, :], col0[low : low + 1, :]
-                b, d = col1[top : top + 1, :], col1[low : low + 1, :]
-                inverse = 1.0 / (a * d - b * c)
-                a, b, c, d = a * inverse, b * inverse, c * inverse, d * inverse
-
-                def step(matrix):
-                    row0, row1 = matrix[top : top + 1, :], matrix[low : low + 1, :]
-                    new0 = d * row0 - b * row1
-                    new1 = a * row1 - c * row0
-                    matrix = matrix - col0 * new0 - col1 * new1
-                    return jnp.where(
-                        row == top, new0, jnp.where(row == low, new1, matrix)
+            rows = [
+                jnp.broadcast_to(parts[home][at + j : at + j + 1, :], spread)
+                for j in range(4)
+            ]
+            e = {}
+            for x in range(4):
+                for y in range(x, 4):
+                    e[x, y] = jnp.broadcast_to(
+                        cols[y][home][at + x : at + x + 1, :], spread
                     )
-
-                if pair == 0:
-                    cols[2], cols[3] = step(cols[2]), step(cols[3])
-                system = step(system)
-        return system
+            inverse = 1.0 / (e[0, 0] * e[1, 1] - e[0, 1] * e[0, 1])
+            a, b, d = e[1, 1] * inverse, -e[0, 1] * inverse, e[0, 0] * inverse
+            t02 = a * e[0, 2] + b * e[1, 2]
+            t03 = a * e[0, 3] + b * e[1, 3]
+            t12 = b * e[0, 2] + d * e[1, 2]
+            t13 = b * e[0, 3] + d * e[1, 3]
+            s22 = e[2, 2] - (e[0, 2] * t02 + e[1, 2] * t12)
+            s23 = e[2, 3] - (e[0, 2] * t03 + e[1, 2] * t13)
+            s33 = e[3, 3] - (e[0, 3] * t03 + e[1, 3] * t13)
+            inverse = 1.0 / (s22 * s33 - s23 * s23)
+            low2 = rows[2] - (t02 * rows[0] + t12 * rows[1])
+            low3 = rows[3] - (t03 * rows[0] + t13 * rows[1])
+            new2 = (s33 * low2 - s23 * low3) * inverse
+            new3 = (s22 * low3 - s23 * low2) * inverse
+            new0 = (a * rows[0] + b * rows[1]) - (t02 * new2 + t03 * new3)
+            new1 = (b * rows[0] + d * rows[1]) - (t12 * new2 + t13 * new3)
+            news = [new0, new1, new2, new3]
+            parts = [
+                parts[v]
+                - (cols[2][v] * new2 + cols[3][v] * new3)
+                - (cols[0][v] * new0 + cols[1][v] * new1)
+                for v in range(groups)
+            ]
+            for j in range(4):
+                parts[home] = jnp.where(row8 == at + j, news[j], parts[home])
+        return jnp.concatenate(parts, axis=0)
 
     def mean_trace(gram):
         return jnp.sum(
@@ -276,7 +295,7 @@
         for k in range(trials_here):
             proj_all[sweep, my_trial, k] = projected[
                 :, k * neurons_here : (k + 1) * neurons_here
-            ]
+            ].astype(jnp.bfloat16)
         mine = proj_all.at[sweep, my_trial]
         send_all(mine, mine, trial_devices, trial_peer, sends[0], receives[0])
         time_gram = split_gram(time_now)
@@ -291,7 +310,8 @@
         wait_bytes(others, receives[0])
 
         blocks = [
-            proj_all[sweep, k // trials_here, k % trials_here] for k in range(trials)
+            proj_all[sweep, k // trials_here, k % trials_here].astype(jnp.float32)
+            for k in range(trials)
         ]
         terms = jnp.zeros((comps, neurons_here), jnp.float32)
         for k in range(trials):
@@ -529,7 +549,9 @@
             pltpu.VMEM((comps, timepoints), f32),
             pltpu.VMEM((trials_here, comps), f32),
             pltpu.VMEM((trial_devices, comps, LANES), f32),
-            pltpu.VMEM((SWEEPS, trial_devices, trials_here, comps, neurons_here), f32),
+            pltpu.VMEM(
+                (SWEEPS, trial_devices, trials_here, comps, neurons_here), jnp.bfloat16
+            ),
             pltpu.VMEM((SWEEPS, neuron_devices, comps // 2, LANES), f32),
             pltpu.VMEM((tiles, ROWS, LANES), f32),
             pltpu.VMEM((devices, ROWS, LANES), f32),

time: 54 us -> 55.9 us (1.035)
  Pallas kernels: 53.3 us -> 55.1 us
    pallas_call x1, Pallas kernels: 51.1 us -> 53 us  [per_device(): pl.pallas_call(functools.partial(kernel, neuron_devices, trial_devices),...]
where the time goes in v4:
time: 55.9 us; the launch traced here: 55.8 us
  Pallas kernels  55.1 us (99%)
  between operations  0.64 us (1%)
    pallas_call x1, Pallas kernels, per_device(): pl.pallas_call(functools.partial(kernel, neuron_devices, trial_devices),...  53 us
    pallas_call x1, Pallas kernels, per_device(): pl.pallas_call(keep, out_shape=tuple((jax.ShapeDtypeStruct(r.shape, f32)...  2.15 us

profile of v4, /device:TPU:0, one launch (start us, length us, event | category | flops | bytes accessed | tf_op | source)
XLA Modules:
  0.0 55.8 jit_solution(7690748198927050246)
XLA Ops:
  0.6 53.0 %shard_map.58 = (f32[32,128]{1,0:T(8,128)}, f32[32,32]{1,0:T(8,128)}, f32[2,32]{1,0:T(2,128)}) custom-call(bf16[2,128,1024]{2,1,0:T(8,128)(2,1)} %tensor_hbm.1, f32[32,1024]{1,0:T(8,128)} %time_hbm.1, f32[2,32]{1,0:T(2,128)} %bitcast.2), custom_call_target="tpu_custom_call" | custom-call | tf_op jit(solution)/shard_map/pallas_call | solution.py:538
  53.6 2.2 %shard_map.59 = (f32[32,128]{1,0:T(8,128)}, f32[32,32]{1,0:T(8,128)}, f32[2,32]{1,0:T(2,128)}) custom-call(f32[32,128]{1,0:T(8,128)} %get-tuple-element.9.neuron_in, f32[32,32]{1,0:T(8,128)} %get-tuple-element.10.time_in, f32[2,32]{1,0:T(2,128)} %get-tuple-element.11.trial_in), custom_call_target="tpu_custom_call" | custom-call | tf_op jit(solution)/shard_map/pallas_call | solution.py:576

commit v5 on v3

--- a/solution.py
+++ b/solution.py
@@ -14,7 +14,6 @@
 LANES = 128
 ROWS = 8
 MESH = pl.DeviceIdType.MESH
-EXACT = lax.Precision.HIGHEST
 NT = (((1,), (1,)), ((), ()))
 
 
@@ -135,13 +134,9 @@
     in_low = (lane >= 2 * comps) & (lane < 3 * comps)
     in_terms = (lane >= comps) & (lane < comps + trials)
 
-    def wide_gram(matrix):
-        padded = jnp.concatenate(
-            [matrix, jnp.zeros((LANES - comps, matrix.shape[1]), matrix.dtype)], axis=0
-        )
-        return lax.dot_general(
-            matrix, padded, NT, precision=EXACT, preferred_element_type=jnp.float32
-        )
+    def widen(gram):
+        blank = jnp.zeros((comps, LANES - comps), jnp.float32)
+        return jnp.concatenate([gram, blank], axis=1)
 
     def split(matrix):
         high = matrix.astype(jnp.bfloat16)
@@ -151,13 +146,8 @@
         high, low = split(matrix)
         left = jnp.concatenate([high, low, high], axis=1)
         right = jnp.concatenate([high, high, low], axis=1)
-        blank = jnp.zeros((LANES - comps, right.shape[1]), jnp.bfloat16)
-        return lax.dot_general(
-            left,
-            jnp.concatenate([right, blank], axis=0),
-            NT,
-            preferred_element_type=jnp.float32,
-        )
+        gram = lax.dot_general(left, right, NT, preferred_element_type=jnp.float32)
+        return widen(gram)
 
     def eliminate(system):
         for k in range(0, comps, 4):
@@ -285,7 +275,7 @@
             wait_bytes(others, trial_sem.at[1])
             wait_bytes(others, trial_sem.at[0])
             trial_wide = jnp.sum(trial_all[...], axis=0)
-            trial_gram = wide_gram(trial_wide)
+            trial_gram = split_gram(trial_wide)
         inverse = inverse_of(trial_gram * time_gram)
         others = proj_all.at[sweep, pl.ds(0, trial_devices - 1)]
         wait_bytes(others, receives[0])
@@ -397,7 +387,7 @@
                 ).start()
 
             each(1, trial_devices, start_share)
-        trial_gram = wide_gram(trial_wide)
+        trial_gram = split_gram(trial_wide)
         inverse = inverse_of(neuron_gram * trial_gram)
         wait_bytes(others, sends[1])
 

time: 54 us -> 54 us (level)
  no operation moved by 1% of the time
where the time goes in v5:
time: 54 us; the launch traced here: 53.9 us
  Pallas kernels  53.2 us (99%)
  between operations  0.64 us (1%)
    pallas_call x1, Pallas kernels, per_device(): pl.pallas_call(functools.partial(kernel, neuron_devices, trial_devices),...  51.1 us
    pallas_call x1, Pallas kernels, per_device(): pl.pallas_call(keep, out_shape=tuple((jax.ShapeDtypeStruct(r.shape, f32)...  2.15 us

profile of v5, /device:TPU:0, one launch (start us, length us, event | category | flops | bytes accessed | tf_op | source)
XLA Modules:
  0.0 53.9 jit_solution(1122792533621775094)
XLA Ops:
  0.6 51.1 %shard_map.58 = (f32[32,128]{1,0:T(8,128)}, f32[32,32]{1,0:T(8,128)}, f32[2,32]{1,0:T(2,128)}) custom-call(bf16[2,128,1024]{2,1,0:T(8,128)(2,1)} %tensor_hbm.1, f32[32,1024]{1,0:T(8,128)} %time_hbm.1, f32[2,32]{1,0:T(2,128)} %bitcast.2), custom_call_target="tpu_custom_call" | custom-call | tf_op jit(solution)/shard_map/pallas_call | solution.py:508
  51.7 2.2 %shard_map.59 = (f32[32,128]{1,0:T(8,128)}, f32[32,32]{1,0:T(8,128)}, f32[2,32]{1,0:T(2,128)}) custom-call(f32[32,128]{1,0:T(8,128)} %get-tuple-element.9.neuron_in, f32[32,32]{1,0:T(8,128)} %get-tuple-element.10.time_in, f32[2,32]{1,0:T(2,128)} %get-tuple-element.11.trial_in), custom_call_target="tpu_custom_call" | custom-call | tf_op jit(solution)/shard_map/pallas_call | solution.py:544
